TPU v7x, 128 devices: a whole 4x4x4 slice. The times are simulated.
128 devices in a mesh: pipe: 4 (over y_lo, core), dp: 32 (over y_hi, z, x).
Axes of the slice: x: 4, y: 4 (y_hi: 2, y_lo: 2; y = y_hi * 2 + y_lo), z: 4, core: 2. Of those that a mesh axis runs over, the one named last changes fastest.
Arguments:
- stash: bfloat16 [4, 2, 5120, 6144], P('pipe', None, 'dp'), may hold values from -6 to 6
- attn: bfloat16 [4, 2, 32, 6, 160, 160], P('pipe', None, 'dp'), may hold values from 0 to 0.03930664
- w_value: bfloat16 [4, 6144, 768], P('pipe'), may hold values from -0.078125 to 0.078125
- w_out: bfloat16 [4, 768, 6144], P('pipe'), may hold values from -0.21875 to 0.21875
- out_grad: bfloat16 [2, 5120, 6144], P(None, 'dp', 'pipe'), may hold values from -6 to 6
- order: int32 [2], replicated, may hold values from 0 to 1, each once
- check_rows: int32 [8, 6144], replicated, may hold values from -3 to 3
Outputs:
- grad_value: float32 [4, 6144, 768], P('pipe', 'dp')
- grad_out_t: float32 [4, 6144, 768], P('pipe', 'dp')
- checksums: float32 [4, 2, 8, 768], P('pipe')
- input_grad: bfloat16 [2, 5120, 6144], P(None, 'dp', 'pipe')
Inputs may be any that keep to these rules, and one draw needn't show every extreme that they name: `order`: a permutation of the micro-batches.
All inputs are finite; a program needn't handle non-finite values.
Results may differ from a plain program's by a relative error of at most 0.022.
Values may be sent and summed in bfloat16 or wider, within the bound.
No kernel may reach another device: no remote copies, remote signals or barrier semaphores. Data moves between devices by JAX's collectives and lax.ppermute only.
A program may use at most 192 MiB of HBM per device.

v0:
```python
import jax
import jax.numpy as jnp
from jax import lax
from jax.sharding import PartitionSpec as P


def passed_along(block, axis, distance):
    devices = range(lax.axis_size(axis))
    route = [(i - distance, i) for i in devices if i - distance in devices]
    return lax.ppermute(block, axis, route)


def from_root(array, axis, root):
    mine = lax.axis_index(axis) == root
    return lax.psum(jnp.where(mine, array, jnp.zeros_like(array)), axis)


def on_device(stash, attn, w_value, w_out, out_grad, order, check_rows):
    npipe = lax.axis_size("pipe")
    section = lax.axis_index("pipe")
    inputs = stash[0]
    probs = attn[0][:, 0]
    wv = w_value[0]
    wo = w_out[0]
    micro = inputs.shape[0]
    seq = inputs.shape[1]
    width = inputs.shape[2]
    inner = wv.shape[1]
    heads = probs.shape[1]
    head_dim = inner // heads
    grad_scale = jnp.float32((micro * seq * lax.axis_size("dp")) ** (-0.5))
    check_scale = jnp.float32(width ** (-0.5))
    causal = (jnp.arange(seq)[:, None] >= jnp.arange(seq)[None, :]).astype(jnp.bfloat16)
    top_grad = lax.all_gather(out_grad, "pipe", axis=2, tiled=True)

    def backward_step(operands):
        xm, pm, dy = operands
        weights = pm * causal
        values = jnp.dot(xm, wv, preferred_element_type=jnp.float32).astype(jnp.bfloat16)
        context = jnp.einsum(
            "hij,jhd->ihd",
            weights,
            values.reshape(seq, heads, head_dim),
            preferred_element_type=jnp.float32,
        )
        context = context.reshape(seq, inner).astype(jnp.bfloat16)
        dctx = jnp.dot(dy, wo.T, preferred_element_type=jnp.float32).astype(jnp.bfloat16)
        dvals = jnp.einsum(
            "hij,ihd->jhd",
            weights,
            dctx.reshape(seq, heads, head_dim),
            preferred_element_type=jnp.float32,
        )
        dvals = dvals.reshape(seq, inner).astype(jnp.bfloat16)
        dx = (
            dy.astype(jnp.float32) + jnp.dot(dvals, wv.T, preferred_element_type=jnp.float32)
        ).astype(jnp.bfloat16)
        return (context, dvals, dx)

    def skip_step(operands):
        return (
            jnp.zeros((seq, inner), jnp.bfloat16),
            jnp.zeros((seq, inner), jnp.bfloat16),
            jnp.zeros((seq, width), jnp.bfloat16),
        )

    ctx_store = jnp.zeros((micro, seq, inner), jnp.bfloat16)
    dv_store = jnp.zeros((micro, seq, inner), jnp.bfloat16)
    dy_store = jnp.zeros((micro, seq, width), jnp.bfloat16)
    dx_store = jnp.zeros((micro, seq, width), jnp.bfloat16)
    incoming = jnp.zeros((seq, width), jnp.bfloat16)
    last_turn = micro + npipe - 2
    for turn in range(micro + npipe - 1):
        step = turn - (npipe - 1 - section)
        valid = jnp.logical_and(step >= 0, step < micro)
        slot = jnp.clip(step, 0, micro - 1)
        batch = order[slot]
        dy = jnp.where(
            section == npipe - 1, lax.dynamic_index_in_dim(top_grad, slot, 0, False), incoming
        )
        xm = lax.dynamic_index_in_dim(inputs, batch, 0, False)
        pm = lax.dynamic_index_in_dim(probs, batch, 0, False)
        context, dvals, dx = lax.cond(valid, backward_step, skip_step, (xm, pm, dy))
        ctx_store = jnp.where(
            valid, lax.dynamic_update_index_in_dim(ctx_store, context, batch, 0), ctx_store
        )
        dv_store = jnp.where(
            valid, lax.dynamic_update_index_in_dim(dv_store, dvals, batch, 0), dv_store
        )
        dy_store = jnp.where(
            valid, lax.dynamic_update_index_in_dim(dy_store, dy, batch, 0), dy_store
        )
        dx_store = jnp.where(
            valid, lax.dynamic_update_index_in_dim(dx_store, dx, slot, 0), dx_store
        )
        if turn < last_turn:
            incoming = passed_along(dx, "pipe", -1)
    x_flat = inputs.reshape(micro * seq, width)
    dv_flat = dv_store.reshape(micro * seq, inner)
    dy_flat = dy_store.reshape(micro * seq, width)
    ctx_flat = ctx_store.reshape(micro * seq, inner)
    contract = (((0,), (0,)), ((), ()))
    ck_float = check_rows.astype(jnp.float32)
    rows = width // lax.axis_size("dp")
    columns = x_flat
    grad_v = lax.psum_scatter(
        (
            lax.dot_general(columns, dv_flat, contract, preferred_element_type=jnp.float32)
            * grad_scale
        ).astype(jnp.bfloat16),
        "dp",
        scatter_dimension=0,
        tiled=True,
    ).astype(jnp.float32)
    columns = dy_flat
    grad_o = lax.psum_scatter(
        (
            lax.dot_general(columns, ctx_flat, contract, preferred_element_type=jnp.float32)
            * grad_scale
        ).astype(jnp.bfloat16),
        "dp",
        scatter_dimension=0,
        tiled=True,
    ).astype(jnp.float32)
    first_row = lax.axis_index("dp") * rows
    ck_part = lax.dynamic_slice_in_dim(ck_float, first_row, rows, 1)
    local_checks = check_scale * jnp.stack(
        [
            jnp.dot(ck_part, grad_v, precision=lax.Precision.HIGHEST),
            jnp.dot(ck_part, grad_o, precision=lax.Precision.HIGHEST),
        ]
    )
    check_sum = lax.psum(local_checks, "dp")
    first_grads = from_root(dx_store, "pipe", 0)
    share = width // npipe
    own_part = lax.dynamic_slice_in_dim(first_grads, section * share, share, 2)
    return (grad_v[None], grad_o[None], check_sum[None], own_part)


def solution(mesh):
    return jax.shard_map(
        on_device,
        mesh=mesh,
        in_specs=(
            P("pipe", None, "dp", None),
            P("pipe", None, "dp", None, None, None),
            P("pipe", None, None),
            P("pipe", None, None),
            P(None, "dp", "pipe"),
            P(),
            P(),
        ),
        out_specs=(
            P("pipe", "dp", None),
            P("pipe", "dp", None),
            P("pipe", None, None, None),
            P(None, "dp", "pipe"),
        ),
        check_vma=False,
    )
```

profile of v0, /device:TPU:16, one launch (start us, length us, event | category | flops | bytes accessed | tf_op | source)
XLA Modules:
  0.0 1039.1 jit_solution(13033466347937102646)
XLA Ops:
  8.0 1.5 fusion.131
  11.5 44.0 %all-gather.2.cloned.1.call-done = bf16[2,160,6144]{2,1,0:T(8,128)(2,1)} async-done(((bf16[2,160,1536]{2,1,0:T(8,128)(2,1)}), bf16[2,160,6144]{2,1,0:T(8,128)(2,1)}) %all-gather.2.cloned.1.call-update) | async-done | bytes 3932176 | tf_op jit(solution)/shard_map/all_gather | solution.py:34
  55.5 2.5 broadcast.104.clone
  57.9 4.3 select_dynamic-update-slice_fusion.5
  62.5 1.8 conditional.5
  62.5 1.6 broadcast.92
  64.4 1.3 collective-permute-start
  67.5 3.3 collective-permute-done
  70.8 5.2 fusion.125
  76.1 3.2 conditional.6
  76.1 1.5 broadcast.94
  77.6 1.5 broadcast_in_dim.112
  79.3 1.3 collective-permute-start.1
  86.4 19.1 %collective-permute-done.1 = bf16[160,6144]{1,0:T(8,128)(2,1)S(1)} collective-permute-done((bf16[160,6144]{1,0:T(8,128)(2,1)}, bf16[160,6144]{1,0:T(8,128)(2,1)S(1)}, u32[]{:S(2)}, u32[]{:S(2)}) %collective-permute-start.1) | collective-permute-done | bytes 1966112 | tf_op jit(solution)/shard_map/ppermute | solution.py:10
  105.5 1.3 copy-done.14
  106.8 5.4 fusion.124
  112.2 0.8 copy-done.2
  112.9 4.6 conditional.7
  112.9 1.5 broadcast.95
  114.5 1.5 broadcast_in_dim.115
  117.6 1.4 collective-permute-start.2
  119.0 2.4 broadcast.104
  121.4 1.7 select_dynamic-update-slice_fusion.4
  123.1 3.9 select_dynamic-update-slice_fusion.3
  127.0 53.4 %collective-permute-done.2 = bf16[160,6144]{1,0:T(8,128)(2,1)S(1)} collective-permute-done((bf16[160,6144]{1,0:T(8,128)(2,1)}, bf16[160,6144]{1,0:T(8,128)(2,1)S(1)}, u32[]{:S(2)}, u32[]{:S(2)}) %collective-permute-start.2) | collective-permute-done | bytes 1966112 | tf_op jit(solution)/shard_map/ppermute | solution.py:10
  180.4 4.1 fusion.123
  184.6 21.8 %conditional.8 = (bf16[160,6144]{1,0:T(8,128)(2,1)}, bf16[1,160,768]{2,1,0:T(8,128)(2,1)}, bf16[1,160,768]{2,1,0:T(8,128)(2,1)S(1)}, bf16[1,160,6144]{2,1,0:T(8,128)(2,1)}) conditional(s32[]{:T(128)} %convert_element_type.329, () %tuple.104, (bf16[160,6144]{1,0:T(8,128)(2,1)S(1)}, bf16[768,6144]{1,0:T(8,128)(2,1)S(1)}, ...), branch_computations={%region_6.7_spmd, %region_7.8_spmd} | conditional | flops 4612700160 | bytes 89258160 | solution.py:83
  185.0 3.9 fusion.81
  189.7 1.5 convolution_convert_fusion.9
  191.3 8.3 fusion.73
  199.6 3.2 copy.226
  202.8 1.8 fusion.82
  205.0 1.0 convert_element_type.298
  206.4 1.3 collective-permute-start.3
  207.7 3.5 select_dynamic-update-slice_fusion.2
  211.2 4.2 select_dynamic-update-slice_fusion.1
  215.4 17.1 %collective-permute-done.3 = bf16[160,6144]{1,0:T(8,128)(2,1)S(1)} collective-permute-done((bf16[160,6144]{1,0:T(8,128)(2,1)}, bf16[160,6144]{1,0:T(8,128)(2,1)S(1)}, u32[]{:S(2)}, u32[]{:S(2)}) %collective-permute-start.3) | collective-permute-done | bytes 1966112 | tf_op jit(solution)/shard_map/ppermute | solution.py:10
  232.6 4.0 fusion.122
  236.6 18.0 %conditional.9 = (bf16[1,160,768]{2,1,0:T(8,128)(2,1)}, bf16[1,160,768]{2,1,0:T(8,128)(2,1)}, bf16[1,160,6144]{2,1,0:T(8,128)(2,1)}) conditional(s32[]{:T(128)} %convert_element_type.330, () %tuple.106, (bf16[1,2,160,6144]{3,2,1,0:T(8,128)(2,1)}, s32[]{:T(128)}, bf16[6144,768]{1,0:T(8,128)(2,1)}, bf16[1,2,1,6,160,160]{5,4,3,2,1,0:T(8,128)(2,1)S(1)}, ...), branch_computations={%region_8.9_spmd, %region_9.10_spmd} | conditional | flops 4612700160 | bytes 98173048 | solution.py:83
  236.8 1.4 copy.102
  238.2 7.1 fusion.105
  245.6 4.6 fusion.97
  250.2 1.8 fusion.106
  252.5 1.0 convert_element_type.303
  253.6 1.0 convert_element_type.307
  254.6 4.1 select_dynamic-update-slice_fusion
  258.7 4.2 broadcast_select_fusion
  263.1 0.8 copy-done.23
  264.4 1.0 select_dynamic-update-slice_fusion.7
  265.4 1.0 select_dynamic-update-slice_fusion.6
  266.4 9.6 fusion.120
  277.1 1.0 select_dynamic-update-slice_fusion.11
  278.1 9.6 fusion.121
  287.7 12.7 %copy.109 = bf16[6144,768]{1,0:T(8,128)(2,1)} copy(bf16[6144,768]{0,1:T(8,128)(2,1)} %fusion.121) | data formatting | bytes 18874368
  300.4 53.4 %all-reduce.2.cloned.1.call-done = bf16[2,160,6144]{2,1,0:T(8,128)(2,1)} async-done(((bf16[2,160,6144]{2,1,0:T(8,128)(2,1)}), bf16[2,160,6144]{2,1,0:T(8,128)(2,1)}) %all-reduce.2.cloned.1.call-update) | async-done | bytes 3932176 | tf_op jit(solution)/shard_map/psum | solution.py:15
  353.9 2.2 constant_dynamic-slice_fusion
  356.1 245.0 %reduce-scatter.5.cloned.1.call-done = bf16[192,768]{1,0:T(8,128)(2,1)} async-done(((bf16[6144,768]{1,0:T(8,128)(2,1)}), bf16[192,768]{1,0:T(8,128)(2,1)}) %reduce-scatter.5.cloned.1.call-update) | async-done | bytes 294928 | tf_op jit(solution)/shard_map/reduce_scatter | solution.py:116
  601.0 1.3 convolution_bitcast_fusion
  602.3 243.8 %reduce-scatter.7.cloned.1.call-done = bf16[192,768]{1,0:T(8,128)(2,1)} async-done(((bf16[6144,768]{1,0:T(8,128)(2,1)}), bf16[192,768]{1,0:T(8,128)(2,1)}) %reduce-scatter.7.cloned.1.call-update) | async-done | bytes 294928
  846.2 1.3 convolution_bitcast_fusion.1
  847.4 181.8 %psum.14 = f32[1,2,8,768]{3,2,1,0:T(8,128)} all-reduce(f32[1,2,8,768]{3,2,1,0:T(8,128)S(1)} %fusion.127), channel_id=1, replica_groups=mesh['pipe'=4,'dp'=32] {'dp'}, use_global_device_ids=true, to_apply=%region_12.13 | all-reduce | flops 12288 | bytes 98304 | tf_op jit(solution)/shard_map/psum | solution.py:133
  1029.2 1.1 copy.110
  1030.4 1.1 copy.103
  1031.5 0.9 bitcast_convert_fusion.1
  (91 shorter events, 7.0 us)
Async XLA Ops:
  7.2 48.3 %all-gather.2.cloned.1.call-start = ((), (), s32[]{:S(2)}) async-start(), calls=%async_computation.2 | async-start | bytes 4915200 | tf_op jit(solution)/shard_map/all_gather | solution.py:34
  7.9 346.0 %all-reduce.2.cloned.1.call-start = ((), (), s32[]{:S(2)}) async-start(), calls=%async_computation.4 | async-start | bytes 7864320 | tf_op jit(solution)/shard_map/psum | solution.py:15
  55.5 7.0 copy-start.1
  57.9 4.6 copy-start.5
  64.3 6.5 copy-start.6
  64.3 11.7 %copy-start.20 = (bf16[1,160,768]{2,1,0:T(8,128)(2,1)}, bf16[1,160,768]{2,1,0:T(8,128)(2,1)S(1)}, u32[]{:S(2)}) copy-start(bf16[1,160,768]{2,1,0:T(8,128)(2,1)S(1)} %get-tuple-element.362) | copy-start | bytes 737284
  64.4 11.7 %copy-start.22 = (bf16[1,160,768]{2,1,0:T(8,128)(2,1)}, bf16[1,160,768]{2,1,0:T(8,128)(2,1)S(1)}, u32[]{:S(2)}) copy-start(bf16[1,160,768]{2,1,0:T(8,128)(2,1)S(1)} %get-tuple-element.353) | copy-start | bytes 737284
  64.4 6.5 collective-permute-start
  79.3 33.6 %copy-start.17 = (bf16[1,160,768]{2,1,0:T(8,128)(2,1)}, bf16[1,160,768]{2,1,0:T(8,128)(2,1)S(1)}, u32[]{:S(2)}) copy-start(bf16[1,160,768]{2,1,0:T(8,128)(2,1)S(1)} %get-tuple-element.355) | copy-start | bytes 737284
  79.3 26.1 %collective-permute-start.1 = (bf16[160,6144]{1,0:T(8,128)(2,1)}, bf16[160,6144]{1,0:T(8,128)(2,1)S(1)}, u32[]{:S(2)}, u32[]{:S(2)}) collective-permute-start(bf16[160,6144]{1,0:T(8,128)(2,1)} %get-tuple-element.356), channel_id=1, source_target_pairs={{32,0},{64,32},{96,64},{33,1},{65,33},{97,65},{34,2},{66,34},{98,6... | collective-permute-start | bytes 5898248 | tf_op jit(solution)/shard_map/ppermute | solution.py:10
  105.5 1.3 copy-start.14
  106.8 6.1 copy-start.2
  117.6 3.8 copy-start.7
  117.6 62.9 %collective-permute-start.2 = (bf16[160,6144]{1,0:T(8,128)(2,1)}, bf16[160,6144]{1,0:T(8,128)(2,1)S(1)}, u32[]{:S(2)}, u32[]{:S(2)}) collective-permute-start(bf16[160,6144]{1,0:T(8,128)(2,1)} %get-tuple-element.358), channel_id=1, source_target_pairs={{32,0},{64,32},{96,64},{33,1},{65,33},{97,65},{34,2},{66,34},{98,6... | collective-permute-start | bytes 5898248 | tf_op jit(solution)/shard_map/ppermute | solution.py:10
  121.4 63.2 %slice-start.12 = ((s8[9437184]{0:T(1024)(128)(4,1)}), s8[4194304]{0:T(1024)(128)(4,1)S(1)}, s32[]{:S(2)}) async-start(s8[9437184]{0:T(1024)(128)(4,1)} %bitcast.268), calls=%async_computation.18 | async-start | bytes 8388608
  123.1 57.3 %copy-start.3 = (bf16[2,160,6144]{2,1,0:T(8,128)(2,1)S(1)}, bf16[2,160,6144]{2,1,0:T(8,128)(2,1)}, u32[]{:S(2)}) copy-start(bf16[2,160,6144]{2,1,0:T(8,128)(2,1)} %all-gather.2.cloned.1.call-done) | copy-start | bytes 11796484
  123.1 61.5 %slice-start.13 = ((s8[9437184]{0:T(1024)(128)(4,1)}), s8[4194304]{0:T(1024)(128)(4,1)S(1)}, s32[]{:S(2)}) async-start(s8[9437184]{0:T(1024)(128)(4,1)} %bitcast.268), calls=%async_computation.19 | async-start | bytes 8388608
  180.4 4.1 slice-start.14
  189.7 13.1 %slice-start.9 = ((s8[9437184]{0:T(1024)(128)(4,1)}), s8[4194304]{0:T(1024)(128)(4,1)S(1)}, s32[]{:S(2)}) async-start(s8[9437184]{0:T(1024)(128)(4,1)} %bitcast.262), calls=%async_computation.15 | async-start | bytes 8388608 | tf_op jit(solution)/shard_map/cond
  191.2 11.5 %slice-start.10 = ((s8[9437184]{0:T(1024)(128)(4,1)}), s8[4194304]{0:T(1024)(128)(4,1)S(1)}, s32[]{:S(2)}) async-start(s8[9437184]{0:T(1024)(128)(4,1)} %bitcast.262), calls=%async_computation.16 | async-start | bytes 8388608 | tf_op jit(solution)/shard_map/cond
  191.3 11.5 %slice-start.11 = ((s8[9437184]{0:T(1024)(128)(4,1)}), s8[1048576]{0:T(1024)(128)(4,1)S(1)}, s32[]{:S(2)}) async-start(s8[9437184]{0:T(1024)(128)(4,1)} %bitcast.262), calls=%async_computation.17 | async-start | bytes 2097152 | tf_op jit(solution)/shard_map/cond
  199.6 3.2 copy-start.11
  202.8 1.8 copy-start.28
  206.4 9.0 copy-start.24
  206.4 26.1 %collective-permute-start.3 = (bf16[160,6144]{1,0:T(8,128)(2,1)}, bf16[160,6144]{1,0:T(8,128)(2,1)S(1)}, u32[]{:S(2)}, u32[]{:S(2)}) collective-permute-start(bf16[160,6144]{1,0:T(8,128)(2,1)} %get-tuple-element.360), channel_id=1, source_target_pairs={{32,0},{64,32},{96,64},{33,1},{65,33},{97,65},{34,2},{66,34},{98,6... | collective-permute-start | bytes 5898248 | tf_op jit(solution)/shard_map/ppermute | solution.py:10
  211.2 21.4 %copy-start.4 = (bf16[2,160,6144]{2,1,0:T(8,128)(2,1)S(1)}, bf16[2,160,6144]{2,1,0:T(8,128)(2,1)}, u32[]{:S(2)}) copy-start(bf16[2,160,6144]{2,1,0:T(8,128)(2,1)} %all-gather.2.cloned.1.call-done) | copy-start | bytes 11796484
  238.2 7.1 copy-start.13
  238.2 7.4 copy-start
  245.6 4.6 copy-start.12
  262.9 0.9 copy-start.23
  262.9 1.1 copy-start.21
  262.9 1.2 copy-start.18
  263.0 338.1 %reduce-scatter.5.cloned.1.call-start = ((), (), s32[]{:S(2)}) async-start(), calls=%async_computation.3 | async-start | bytes 9732096 | tf_op jit(solution)/shard_map/reduce_scatter | solution.py:116
  276.0 1.0 copy-start.25
  276.1 570.1 %reduce-scatter.7.cloned.1.call-start = ((), (), s32[]{:S(2)}) async-start(), calls=%async_computation.5 | async-start | bytes 9732096
  601.0 430.5 %copy-start.16 = (bf16[192,768]{1,0:T(8,128)(2,1)S(1)}, bf16[192,768]{1,0:T(8,128)(2,1)}, u32[]{:S(2)}) copy-start(bf16[192,768]{1,0:T(8,128)(2,1)} %reduce-scatter.5.cloned.1.call-done) | copy-start | bytes 884740
Sparse Core Ops, SparseCore 0:
  9.7 45.7 all-gather.1
  263.1 90.7 all-reduce.1
  359.2 241.7 reduce-scatter.4
  606.2 239.8 reduce-scatter.6
where the time goes:
time: 1050 us; the launch traced here: 1040 us
  waiting for transfers between devices  680 us (65%)
  blocking collectives  182 us (17%)
  matrix products  51.8 us (5%)
  other arithmetic  49.2 us (5%)
  local copies, waits for them, and re-layouts  45.9 us (4%)
  between operations  23.8 us (2%)
    reduce_scatter x1, waiting for transfers between devices, on_device(): lax.psum_scatter((lax.dot_general(columns, ctx_flat, contract, preferred_...  245 us
    unnamed x5, waiting for transfers between devices  245 us
    psum x1, blocking collectives, on_device(): check_sum = lax.psum(local_checks, 'dp')  182 us
    ppermute x4, waiting for transfers between devices, passed_along(): return lax.ppermute(block, axis, route)  93 us
    psum x1, waiting for transfers between devices, from_root(): return lax.psum(jnp.where(mine, array, jnp.zeros_like(array)), axis)  53.4 us
    all_gather x1, waiting for transfers between devices, on_device(): top_grad = lax.all_gather(out_grad, 'pipe', axis=2, tiled=True)  44 us
    select_n x5, other arithmetic, on_device(): jnp.where(valid, lax.dynamic_update_index_in_dim(dy_store, dy, batch, 0),...  23 us
  transfers between devices with their start and end apart: 8, of which 8 were waited for; matrix products, arithmetic and copies ran while one was open for 5% of the time, Pallas kernels for 0%

commit v1 on v0

--- a/solution.py
+++ b/solution.py
@@ -130,7 +130,7 @@
             jnp.dot(ck_part, grad_o, precision=lax.Precision.HIGHEST),
         ]
     )
-    check_sum = lax.psum(local_checks, "dp")
+    check_sum = jnp.sum(lax.all_gather(local_checks, "dp"), axis=0)
     first_grads = from_root(dx_store, "pipe", 0)
     share = width // npipe
     own_part = lax.dynamic_slice_in_dim(first_grads, section * share, share, 2)

time: 1050 us -> 945 us (0.900)
  blocking collectives: 182 us -> 0 us
  waiting for transfers between devices: 680 us -> 760 us
    psum x1 -> x0, blocking collectives: 182 us -> none  [on_device(): check_sum = lax.psum(local_checks, 'dp')]
    all_gather x0 -> x1, waiting for transfers between devices: none -> 65.5 us  [on_device(): check_sum = jnp.sum(lax.all_gather(local_checks, 'dp'), axis=0)]
    psum x1, waiting for transfers between devices: 53.4 us -> 86.6 us  [from_root(): return lax.psum(jnp.where(mine, array, jnp.zeros_like(array)), axis)]
    reduce_scatter x1, waiting for transfers between devices: 245 us -> 213 us  [on_device(): lax.psum_scatter((lax.dot_general(columns, ctx_flat, contract, preferred_...]
    ppermute x4, waiting for transfers between devices: 93 us -> 106 us  [passed_along(): return lax.ppermute(block, axis, route)]
    select_n x5, other arithmetic: 17.4 us -> 6.56 us  [on_device(): jnp.where(valid, lax.dynamic_update_index_in_dim(dx_store, dx, slot, 0),...]
    unnamed x43 -> x37, local copies, waits for them, and re-layouts: 18.5 us -> 21.3 us
    unnamed x5 -> x6, waiting for transfers between devices: 245 us -> 245 us
  transfers between devices with their start and end apart: 8 -> 9, of which waited for: 8 -> 9; matrix products, arithmetic and copies ran while one was open for 5% -> 5% of each run, Pallas kernels for 0% -> 0%
where the time goes in v1:
time: 945 us; the launch traced here: 933 us
  waiting for transfers between devices  760 us (80%)
  matrix products  54.1 us (6%)
  local copies, waits for them, and re-layouts  47.3 us (5%)
  other arithmetic  40.7 us (4%)
  between operations  24.5 us (3%)
    unnamed x6, waiting for transfers between devices  245 us
    reduce_scatter x1, waiting for transfers between devices, on_device(): lax.psum_scatter((lax.dot_general(columns, ctx_flat, contract, preferred_...  213 us
    ppermute x4, waiting for transfers between devices, passed_along(): return lax.ppermute(block, axis, route)  106 us
    psum x1, waiting for transfers between devices, from_root(): return lax.psum(jnp.where(mine, array, jnp.zeros_like(array)), axis)  86.6 us
    all_gather x1, waiting for transfers between devices, on_device(): check_sum = jnp.sum(lax.all_gather(local_checks, 'dp'), axis=0)  65.5 us
    all_gather x1, waiting for transfers between devices, on_device(): top_grad = lax.all_gather(out_grad, 'pipe', axis=2, tiled=True)  44 us
    select_n x5, other arithmetic, on_device(): jnp.where(valid, lax.dynamic_update_index_in_dim(dy_store, dy, batch, 0),...  24.8 us
    unnamed x37, local copies, waits for them, and re-layouts  21.3 us
  transfers between devices with their start and end apart: 9, of which 9 were waited for; matrix products, arithmetic and copies ran while one was open for 5% of the time, Pallas kernels for 0%

profile of v1, /device:TPU:16, one launch (start us, length us, event | category | flops | bytes accessed | tf_op | source)
XLA Modules:
  0.0 933.5 jit_solution(16920493250119993928)
XLA Ops:
  8.0 1.5 fusion.130
  11.5 44.0 %all-gather.3.cloned.1.call-done = bf16[2,160,6144]{2,1,0:T(8,128)(2,1)} async-done(((bf16[2,160,1536]{2,1,0:T(8,128)(2,1)}), bf16[2,160,6144]{2,1,0:T(8,128)(2,1)}) %all-gather.3.cloned.1.call-update) | async-done | bytes 3932176 | tf_op jit(solution)/shard_map/all_gather | solution.py:34
  55.5 2.5 broadcast.111.clone
  57.9 4.3 select_dynamic-update-slice_fusion.5
  62.5 3.2 conditional.5
  62.5 1.6 broadcast.99
  65.7 1.3 collective-permute-start
  69.1 3.1 collective-permute-done
  72.2 5.2 fusion.125
  77.4 3.2 conditional.6
  77.4 1.5 broadcast.101
  78.9 1.5 broadcast_in_dim.112
  80.7 1.3 collective-permute-start.1
  84.1 22.7 %collective-permute-done.1 = bf16[160,6144]{1,0:T(8,128)(2,1)S(1)} collective-permute-done((bf16[160,6144]{1,0:T(8,128)(2,1)}, bf16[160,6144]{1,0:T(8,128)(2,1)S(1)}, u32[]{:S(2)}, u32[]{:S(2)}) %collective-permute-start.1) | collective-permute-done | bytes 1966112 | tf_op jit(solution)/shard_map/ppermute | solution.py:10
  106.8 1.3 copy-done.15
  108.1 5.4 fusion.124
  113.5 0.8 copy-done.2
  114.3 4.8 conditional.7
  114.3 1.5 broadcast.102
  115.8 1.5 broadcast_in_dim.115
  118.0 0.7 broadcast_in_dim.114.clone
  119.1 1.3 collective-permute-start.2
  122.3 58.6 %collective-permute-done.2 = bf16[160,6144]{1,0:T(8,128)(2,1)S(1)} collective-permute-done((bf16[160,6144]{1,0:T(8,128)(2,1)}, bf16[160,6144]{1,0:T(8,128)(2,1)S(1)}, u32[]{:S(2)}, u32[]{:S(2)}) %collective-permute-start.2) | collective-permute-done | bytes 1966112 | tf_op jit(solution)/shard_map/ppermute | solution.py:10
  180.9 1.3 copy-done.16
  182.2 5.2 fusion.123
  187.4 23.8 %conditional.8 = (bf16[160,6144]{1,0:T(8,128)(2,1)}, bf16[1,160,768]{2,1,0:T(8,128)(2,1)S(1)}, bf16[1,160,768]{2,1,0:T(8,128)(2,1)S(1)}, bf16[1,160,6144]{2,1,0:T(8,128)(2,1)}) conditional(s32[]{:T(128)} %convert_element_type.329, () %tuple.104, (bf16[160,6144]{1,0:T(8,128)(2,1)S(1)}, bf16[768,6144]{1,0:T(8,128)(2,1)}, ...), branch_computations={%region_6.7_spmd, %region_7.8_spmd} | conditional | flops 4612700160 | bytes 89258160 | solution.py:83
  187.6 6.9 fusion.81
  195.3 1.4 convolution_convert_fusion.9
  196.7 8.4 fusion.73
  205.1 3.2 copy.226
  208.3 1.8 fusion.82
  211.2 1.3 collective-permute-start.3
  215.7 21.7 %collective-permute-done.3 = bf16[160,6144]{1,0:T(8,128)(2,1)S(1)} collective-permute-done((bf16[160,6144]{1,0:T(8,128)(2,1)}, bf16[160,6144]{1,0:T(8,128)(2,1)S(1)}, u32[]{:S(2)}, u32[]{:S(2)}) %collective-permute-start.3) | collective-permute-done | bytes 1966112 | tf_op jit(solution)/shard_map/ppermute | solution.py:10
  237.4 1.3 copy-done.14
  238.7 4.6 fusion.122
  243.3 18.0 %conditional.9 = (bf16[1,160,768]{2,1,0:T(8,128)(2,1)}, bf16[1,160,768]{2,1,0:T(8,128)(2,1)}, bf16[1,160,6144]{2,1,0:T(8,128)(2,1)}) conditional(s32[]{:T(128)} %convert_element_type.330, () %tuple.106, (bf16[1,2,160,6144]{3,2,1,0:T(8,128)(2,1)}, s32[]{:T(128)}, bf16[6144,768]{1,0:T(8,128)(2,1)}, bf16[1,2,1,6,160,160]{5,4,3,2,1,0:T(8,128)(2,1)S(1)}, ...), branch_computations={%region_8.9_spmd, %region_9.10_spmd} | conditional | flops 4612700160 | bytes 100139184 | solution.py:83
  243.5 1.4 copy.102
  244.9 7.1 fusion.105
  252.3 4.5 fusion.97
  256.9 1.8 fusion.106
  259.2 1.0 convert_element_type.303
  260.3 1.0 convert_element_type.307
  261.2 1.8 select_dynamic-update-slice_fusion.6
  263.1 9.1 fusion.120
  273.2 1.0 select_dynamic-update-slice_fusion.11
  274.2 9.6 %fusion.121 = bf16[6144,768]{0,1:T(8,128)(2,1)} fusion(bf16[320,768]{1,0:T(8,128)(2,1)S(1)} %bitcast.268, bf16[320,6144]{1,0:T(8,128)(2,1)} %bitcast.269), kind=kOutput, calls=%fused_computation.128 | convolution fusion | flops 3029336064 | bytes 13860864 | tf_op jit(solution)/shard_map/dot_general | solution.py:108
  283.8 12.2 %copy.109 = bf16[6144,768]{1,0:T(8,128)(2,1)} copy(bf16[6144,768]{0,1:T(8,128)(2,1)} %fusion.121) | data formatting | bytes 18874368
  296.6 1.0 copy-done.6
  298.1 0.7 select_dynamic-update-slice_fusion.3
  298.8 0.7 select_dynamic-update-slice_fusion.2
  299.6 2.3 select_dynamic-update-slice_fusion.1
  301.9 2.3 select_dynamic-update-slice_fusion
  304.2 2.2 broadcast_select_fusion
  306.5 213.1 %reduce-scatter.5.cloned.1.call-done = bf16[192,768]{1,0:T(8,128)(2,1)} async-done(((bf16[6144,768]{1,0:T(8,128)(2,1)}), bf16[192,768]{1,0:T(8,128)(2,1)}) %reduce-scatter.5.cloned.1.call-update) | async-done | bytes 294928 | tf_op jit(solution)/shard_map/reduce_scatter | solution.py:116
  519.6 1.3 convolution_bitcast_fusion
  520.9 244.0 %reduce-scatter.7.cloned.1.call-done = bf16[192,768]{1,0:T(8,128)(2,1)} async-done(((bf16[6144,768]{1,0:T(8,128)(2,1)}), bf16[192,768]{1,0:T(8,128)(2,1)}) %reduce-scatter.7.cloned.1.call-update) | async-done | bytes 294928
  764.9 1.3 convolution_bitcast_fusion.1
  766.9 86.6 %all-reduce.2.cloned.1.call-done = bf16[2,160,6144]{2,1,0:T(8,128)(2,1)} async-done(((bf16[2,160,6144]{2,1,0:T(8,128)(2,1)}), bf16[2,160,6144]{2,1,0:T(8,128)(2,1)}) %all-reduce.2.cloned.1.call-update) | async-done | bytes 3932176 | tf_op jit(solution)/shard_map/psum | solution.py:15
  853.5 2.2 constant_dynamic-slice_fusion
  855.7 1.1 copy.110
  856.9 1.1 copy.103
  858.0 0.9 bitcast_convert_fusion.1
  858.8 65.5 %all-gather.5.cloned.1.call-done = f32[32,2,8,768]{3,2,1,0:T(8,128)} async-done(((f32[1,2,8,768]{3,2,1,0:T(8,128)}), f32[32,2,8,768]{3,2,1,0:T(8,128)}) %all-gather.5.cloned.1.call-update) | async-done | bytes 1572880 | tf_op jit(solution)/shard_map/all_gather | solution.py:133
  924.4 2.1 reduce_sum.9
  (91 shorter events, 10.0 us)
Async XLA Ops:
  7.2 48.3 %all-gather.3.cloned.1.call-start = ((), (), s32[]{:S(2)}) async-start(), calls=%async_computation.2 | async-start | bytes 4915200 | tf_op jit(solution)/shard_map/all_gather | solution.py:34
  7.9 511.7 %reduce-scatter.5.cloned.1.call-start = ((), (), s32[]{:S(2)}) async-start(), calls=%async_computation.3 | async-start | bytes 9732096 | tf_op jit(solution)/shard_map/reduce_scatter | solution.py:116
  55.5 7.0 copy-start.1
  57.9 4.6 copy-start.4
  65.7 6.5 copy-start.5
  65.7 6.4 collective-permute-start
  80.6 33.6 %copy-start.21 = (bf16[1,160,768]{2,1,0:T(8,128)(2,1)}, bf16[1,160,768]{2,1,0:T(8,128)(2,1)S(1)}, u32[]{:S(2)}) copy-start(bf16[1,160,768]{2,1,0:T(8,128)(2,1)S(1)} %get-tuple-element.363) | copy-start | bytes 737284
  80.7 33.6 %copy-start.22 = (bf16[1,160,768]{2,1,0:T(8,128)(2,1)}, bf16[1,160,768]{2,1,0:T(8,128)(2,1)S(1)}, u32[]{:S(2)}) copy-start(bf16[1,160,768]{2,1,0:T(8,128)(2,1)S(1)} %get-tuple-element.355) | copy-start | bytes 737284
  80.7 26.1 %collective-permute-start.1 = (bf16[160,6144]{1,0:T(8,128)(2,1)}, bf16[160,6144]{1,0:T(8,128)(2,1)S(1)}, u32[]{:S(2)}, u32[]{:S(2)}) collective-permute-start(bf16[160,6144]{1,0:T(8,128)(2,1)} %get-tuple-element.356), channel_id=1, source_target_pairs={{32,0},{64,32},{96,64},{33,1},{65,33},{97,65},{34,2},{66,34},{98,6... | collective-permute-start | bytes 5898248 | tf_op jit(solution)/shard_map/ppermute | solution.py:10
  106.8 1.3 copy-start.15
  108.1 6.1 copy-start.2
  119.1 61.8 %collective-permute-start.2 = (bf16[160,6144]{1,0:T(8,128)(2,1)}, bf16[160,6144]{1,0:T(8,128)(2,1)S(1)}, u32[]{:S(2)}, u32[]{:S(2)}) collective-permute-start(bf16[160,6144]{1,0:T(8,128)(2,1)} %get-tuple-element.358), channel_id=1, source_target_pairs={{32,0},{64,32},{96,64},{33,1},{65,33},{97,65},{34,2},{66,34},{98,6... | collective-permute-start | bytes 5898248 | tf_op jit(solution)/shard_map/ppermute | solution.py:10
  180.9 1.3 copy-start.16
  195.3 13.0 %slice-start.9 = ((s8[9437184]{0:T(1024)(128)(4,1)}), s8[4194304]{0:T(1024)(128)(4,1)S(1)}, s32[]{:S(2)}) async-start(s8[9437184]{0:T(1024)(128)(4,1)} %bitcast.261), calls=%async_computation.16 | async-start | bytes 8388608 | tf_op jit(solution)/shard_map/cond
  196.7 11.6 %slice-start.10 = ((s8[9437184]{0:T(1024)(128)(4,1)}), s8[4194304]{0:T(1024)(128)(4,1)S(1)}, s32[]{:S(2)}) async-start(s8[9437184]{0:T(1024)(128)(4,1)} %bitcast.261), calls=%async_computation.17 | async-start | bytes 8388608 | tf_op jit(solution)/shard_map/cond
  196.7 11.6 %slice-start.11 = ((s8[9437184]{0:T(1024)(128)(4,1)}), s8[1048576]{0:T(1024)(128)(4,1)S(1)}, s32[]{:S(2)}) async-start(s8[9437184]{0:T(1024)(128)(4,1)} %bitcast.261), calls=%async_computation.18 | async-start | bytes 2097152 | tf_op jit(solution)/shard_map/cond
  205.1 3.2 copy-start.11
  208.3 1.8 copy-start.30
  211.2 3.3 copy-start.25
  211.2 3.3 copy-start.27
  211.2 26.1 %collective-permute-start.3 = (bf16[160,6144]{1,0:T(8,128)(2,1)}, bf16[160,6144]{1,0:T(8,128)(2,1)S(1)}, u32[]{:S(2)}, u32[]{:S(2)}) collective-permute-start(bf16[160,6144]{1,0:T(8,128)(2,1)} %get-tuple-element.360), channel_id=1, source_target_pairs={{32,0},{64,32},{96,64},{33,1},{65,33},{97,65},{34,2},{66,34},{98,6... | collective-permute-start | bytes 5898248 | tf_op jit(solution)/shard_map/ppermute | solution.py:10
  214.5 24.2 %copy-start.3 = (bf16[2,160,6144]{2,1,0:T(8,128)(2,1)S(1)}, bf16[2,160,6144]{2,1,0:T(8,128)(2,1)}, u32[]{:S(2)}) copy-start(bf16[2,160,6144]{2,1,0:T(8,128)(2,1)} %all-gather.3.cloned.1.call-done) | copy-start | bytes 11796484
  214.5 1.1 copy-start.26
  215.7 21.7 %copy-start.7 = (bf16[2,160,768]{2,1,0:T(8,128)(2,1)}, bf16[2,160,768]{2,1,0:T(8,128)(2,1)S(1)}, u32[]{:S(2)}) copy-start(bf16[2,160,768]{2,1,0:T(8,128)(2,1)S(1)} %select_dynamic-update-slice_fusion.7) | copy-start | bytes 1474564
  237.4 1.3 copy-start.14
  244.9 7.1 copy-start.13
  244.9 7.4 copy-start
  252.3 4.5 copy-start.18
  252.3 4.5 copy-start.12
  256.9 3.3 copy-start.19
  272.2 0.9 copy-start.28
  272.2 492.7 %reduce-scatter.7.cloned.1.call-start = ((), (), s32[]{:S(2)}) async-start(), calls=%async_computation.6 | async-start | bytes 9732096
  296.1 1.6 copy-start.6
  296.1 557.4 %all-reduce.2.cloned.1.call-start = ((), (), s32[]{:S(2)}) async-start(), calls=%async_computation.5 | async-start | bytes 7864320 | tf_op jit(solution)/shard_map/psum | solution.py:15
  306.5 617.9 %all-gather.5.cloned.1.call-start = ((), (), s32[]{:S(2)}) async-start(), calls=%async_computation.4 | async-start | bytes 1622016 | tf_op jit(solution)/shard_map/all_gather | solution.py:133
  519.6 338.4 %copy-start.20 = (bf16[192,768]{1,0:T(8,128)(2,1)S(1)}, bf16[192,768]{1,0:T(8,128)(2,1)}, u32[]{:S(2)}) copy-start(bf16[192,768]{1,0:T(8,128)(2,1)} %reduce-scatter.5.cloned.1.call-done) | copy-start | bytes 884740
Sparse Core Ops, SparseCore 0:
  9.7 45.7 all-gather.2
  272.4 247.1 reduce-scatter.4
  525.0 239.9 reduce-scatter.6
  767.3 86.1 all-reduce.1
  857.0 67.3 all-gather.4
